TPU v7x, 32 devices: a whole 2x2x4 slice. The times are simulated.
32 devices in a mesh: section: 4 (over x, core), tp: 8 (over z, y).
Axes of the slice: x: 2, y: 2, z: 4, core: 2. Of those that a mesh axis runs over, the one named last changes fastest.
Arguments:
- hidden: bfloat16 [1024, 8192], P(('section', 'tp')), may hold values from -6 to 6
- norm_gain: float32 [4, 8192], P('section'), may hold values from 0.5 to 1.5
- w_query: bfloat16 [4, 8192, 8192], P('section', None, 'tp'), may hold values from -0.125 to 0.125
- w_keyval: bfloat16 [4, 8192, 2048], P('section', None, 'tp'), may hold values from -0.0625 to 0.0625
- w_out: bfloat16 [4, 8192, 8192], P('section', 'tp'), may hold values from -0.25 to 0.25
- kv_pool: bfloat16 [4, 32, 128, 2048], P('section', 'tp'), may hold values from -70 to 70
- page_table: int32 [4, 32], P('section'), may hold values from 0 to 31, as said below
- prefix_len: int32 [4, 4], P('section'), may hold values from 1 to 1024, 2560 in all within a row
- decode_place: int32 [4, 32], P('section'), may hold values from 0 to 31, each once within a row
Outputs:
- handed: bfloat16 [1024, 8192], P(('section', 'tp'))
- decode_cache: bfloat16 [4, 32, 64, 256], P('section', 'tp')
Inputs may be any that keep to these rules, and one draw needn't show every extreme that they name: `page_table`: every page of a section's pool appears once in its page table, and of the pages k * 4 to k * 4 + 3 exactly 1 stand in each request's list. `prefix_len`: some request of every section has exactly 1024 prefix tokens. `decode_place`: every slot appears once for each section.
All inputs are finite; a program needn't handle non-finite values.
Results may differ from a plain program's by a relative error of at most 0.024.
The roundings to bfloat16 on the way count: a program that leaves them out, or rounds other values in their place, can miss the bound.
Values may be sent and summed in bfloat16 or wider, within the bound.
A program may use at most 128 MiB of HBM per device.

v0:
```python
import functools

import jax
import jax.numpy as jnp
from jax import lax
from jax.experimental import pallas as pl
from jax.experimental.pallas import tpu as pltpu
from jax.sharding import PartitionSpec as P

KVH = 8
HD = 128
PAGE = 128
REQ = 4
NEW = 64


rope_theta = 500000.0


def from_behind(value, axis, steps):
    count = lax.axis_size(axis)
    pairs = [(source, (source + steps) % count) for source in range(count)]
    return lax.ppermute(value, axis, pairs)


def rotate(values, positions, dims, apply, head_size):
    rows = values.shape[0]
    cols = values.shape[1]
    inverse = jnp.power(rope_theta, -(dims // 2 * 2).astype(jnp.float32) / head_size)
    angle = positions[:, None].astype(jnp.float32) * inverse[None, :]
    cosine = jnp.cos(angle)[:, 0::2]
    sine = jnp.sin(angle)[:, 0::2]
    pairs = values.reshape(rows, cols // 2, 2)
    even = pairs[:, :, 0]
    odd = pairs[:, :, 1]
    turned = jnp.stack([even * cosine - odd * sine, even * sine + odd * cosine], axis=-1).reshape(
        rows, cols
    )
    return jnp.where(apply[None, :], turned, values)


def attend(qheads, prefix_kv, fresh_kv, lens):
    prefix = prefix_kv.shape[1]
    count = qheads.shape[1]
    scale = HD ** (-0.5)
    score_pre = (
        jnp.einsum(
            "rnhd,rkd->rhnk", qheads, prefix_kv[:, :, :HD], preferred_element_type=jnp.float32
        )
        * scale
    )
    score_new = (
        jnp.einsum(
            "rnhd,rkd->rhnk", qheads, fresh_kv[:, :, :HD], preferred_element_type=jnp.float32
        )
        * scale
    )
    seen_pre = (jnp.arange(prefix, dtype=jnp.int32)[None, :] < lens[:, None])[:, None, None, :]
    npos = jnp.arange(count, dtype=jnp.int32)
    seen_new = (npos[None, :] <= npos[:, None])[None, None, :, :]
    top = jnp.maximum(
        jnp.max(jnp.where(seen_pre, score_pre, -1e30), axis=-1, keepdims=True),
        jnp.max(jnp.where(seen_new, score_new, -1e30), axis=-1, keepdims=True),
    )
    expo_pre = jnp.where(seen_pre, jnp.exp(score_pre - top), 0.0)
    expo_new = jnp.where(seen_new, jnp.exp(score_new - top), 0.0)
    total = jnp.sum(expo_pre, axis=-1, keepdims=True) + jnp.sum(expo_new, axis=-1, keepdims=True)
    weight_pre = (expo_pre / total).astype(jnp.bfloat16)
    weight_new = (expo_new / total).astype(jnp.bfloat16)
    mixed = jnp.einsum(
        "rhnk,rkd->rnhd", weight_pre, prefix_kv[:, :, HD:], preferred_element_type=jnp.float32
    )
    mixed = mixed + jnp.einsum(
        "rhnk,rkd->rnhd", weight_new, fresh_kv[:, :, HD:], preferred_element_type=jnp.float32
    )
    return mixed.astype(jnp.bfloat16)


def local(
    hidden, norm_gain, w_query, w_keyval, w_out, kv_pool, page_table, prefix_len, decode_place
):
    tp_count = lax.axis_size("tp")
    tp_rank = lax.axis_index("tp")
    w_q = w_query[0]
    w_kv = w_keyval[0]
    w_o = w_out[0]
    q_cols = w_q.shape[1]
    kv_cols = w_kv.shape[1]
    rows_dev = hidden.shape[0]
    xf = hidden.astype(jnp.float32)
    meansq = jnp.mean(xf * xf, axis=-1, keepdims=True)
    normed = (xf * lax.rsqrt(meansq + 1e-05) * norm_gain[0][None, :]).astype(jnp.bfloat16)
    project_piece = lax.all_gather(normed, "tp", axis=0, tiled=True)
    projected = jnp.concatenate(
        [
            jnp.dot(project_piece, w_q, preferred_element_type=jnp.float32),
            jnp.dot(project_piece, w_kv, preferred_element_type=jnp.float32),
        ],
        axis=1,
    )
    lens = prefix_len[0]
    positions = (lens[:, None] + jnp.arange(NEW, dtype=jnp.int32)[None, :]).reshape(-1)
    qdims = jnp.arange(q_cols, dtype=jnp.int32)
    query = rotate(projected[:, :q_cols], positions, qdims % HD, qdims >= 0, HD).astype(
        jnp.bfloat16
    )
    kdims = tp_rank * kv_cols + jnp.arange(kv_cols, dtype=jnp.int32)
    keyval = rotate(projected[:, q_cols:], positions, kdims % HD, kdims // HD % 2 == 0, HD).astype(
        jnp.bfloat16
    )
    keyval_all = lax.all_gather(keyval, "tp", axis=1, tiled=True)
    pool_local = kv_pool[0]
    pool_dev = pool_local.shape[0]
    table_flat = page_table[0]
    listed = table_flat.shape[0] // REQ
    prefix = listed * PAGE
    heads_dev = q_cols // HD
    members = tp_count // KVH
    kv_head = tp_rank // members
    by_head = pool_local.reshape(pool_dev, PAGE, KVH, 2 * HD).transpose(2, 0, 1, 3)
    outgoing = jnp.repeat(by_head, members, axis=0)
    received = lax.all_to_all(outgoing, "tp", split_axis=0, concat_axis=0, tiled=True)
    flat_pages = received.reshape(-1, PAGE, 2 * HD)
    prefix_kv = flat_pages[table_flat.reshape(REQ, listed)].reshape(REQ, prefix, 2 * HD)
    fresh_kv = lax.dynamic_slice_in_dim(keyval_all, kv_head * 2 * HD, 2 * HD, 1).reshape(
        REQ, NEW, 2 * HD
    )
    qheads = query.reshape(REQ, NEW, heads_dev, HD)
    attended = attend(qheads, prefix_kv, fresh_kv, lens).reshape(REQ * NEW, q_cols)
    summed = lax.psum(
        jnp.dot(attended, w_o, preferred_element_type=jnp.float32).astype(jnp.bfloat16), "tp"
    ).astype(jnp.float32)
    mine = lax.dynamic_slice_in_dim(summed, tp_rank * rows_dev, rows_dev, 0)
    block = (xf + mine).astype(jnp.bfloat16)
    handed = from_behind(block, "section", 1)
    slots_dev = REQ * KVH // tp_count
    places = decode_place[0]
    units = keyval_all.reshape(REQ, NEW, KVH, 2 * HD)
    unit_ids = jnp.arange(REQ * KVH, dtype=jnp.int32)
    pieces = []
    for slot in range(slots_dev):
        wanted = tp_rank * slots_dev + slot
        unit = jnp.sum(jnp.where(places == wanted, unit_ids, 0))
        request = unit // KVH
        head = unit % KVH
        zero = jnp.zeros((), jnp.int32)
        piece = lax.dynamic_slice(units, (request, zero, head, zero), (1, NEW, 1, 2 * HD))
        pieces.append(piece.reshape(NEW, 2 * HD))
    decode_cache = jnp.stack(pieces, axis=0)[None]
    return (handed, decode_cache)


MESH = pl.DeviceIdType.MESH
CHUNKS = 4
TILE = 256
HALF = 16


def ring_place(t, n):
    z, y = lax.div(t, 2), lax.rem(t, 2)
    return (1 - y) * z + y * (n - 1 - z)


def ring_member(p, n):
    half = n // 2
    far = lax.div(p, half)
    return (1 - far) * (2 * p) + far * (2 * (n - 1 - p) + 1)


def layer_kernel(
    n,
    n_section,
    hidden_ref,
    gain_ref,
    wq_hbm,
    wkv_hbm,
    wo_hbm,
    pool_hbm,
    cos_ref,
    sin_ref,
    table_ref,
    lens_ref,
    place_ref,
    handed_hbm,
    cache_ref,
    xg,
    wq,
    wkv,
    wo,
    pages,
    acc,
    qs,
    fresh,
    kbuf,
    att,
    rs_half,
    rs_full,
    block,
    w_sem,
    own_sem,
    ag_send,
    ag_recv,
    pg_send,
    pg_recv,
    kv_send,
    kv_recv,
    rs_send,
    rs_recv,
    hand_send,
    hand_recv,
):
    sec = lax.axis_index("section")
    me = lax.axis_index("tp")
    rows, width = hidden_ref.shape
    chunk = width // CHUNKS
    q_cols = wq.shape[1]
    heads = q_cols // HD
    pool_dev = pool_hbm.shape[0]
    listed = table_ref.shape[0] // REQ
    prefix = listed * PAGE
    ring = ring_place(me, n)
    next_sec = lax.rem(sec + 1, n_section)
    prev_sec = lax.rem(sec + n_section - 1, n_section)

    def at_ring(offset):
        return ring_member(lax.rem(ring + offset + 2 * n, n), n)

    barrier = pltpu.get_barrier_semaphore()
    for k in range(1, n):
        pl.semaphore_signal(
            barrier, inc=1, device_id=(sec, lax.rem(me + k, n)), device_id_type=MESH
        )
    for other in (next_sec, prev_sec):
        pl.semaphore_signal(barrier, inc=1, device_id=(other, me), device_id_type=MESH)

    loads = []
    for c in range(CHUNKS):
        part = pl.ds(c * chunk, chunk)
        first = pltpu.make_async_copy(wq_hbm.at[part, :], wq.at[part, :], w_sem.at[3 * c])
        second = pltpu.make_async_copy(wkv_hbm.at[part, :], wkv.at[part, :], w_sem.at[3 * c + 1])
        loads.append((first, second))
        first.start()
        second.start()
    out_loads = []
    for c in range(CHUNKS):
        part = pl.ds(c * chunk, chunk)
        out_loads.append(
            pltpu.make_async_copy(wo_hbm.at[:, part], wo.at[:, part], w_sem.at[3 * c + 2])
        )
        out_loads[-1].start()
    pair = 2 * HD
    own_pages = pltpu.make_async_copy(
        pool_hbm.at[:, :, pl.ds(pl.multiple_of(me * pair, pair), pair)],
        pages.at[pl.ds(me * pool_dev, pool_dev)],
        own_sem,
    )
    own_pages.start()

    xf = hidden_ref[...].astype(jnp.float32)
    meansq = jnp.mean(xf * xf, axis=-1, keepdims=True)
    normed = (xf * lax.rsqrt(meansq + 1e-05) * gain_ref[...]).astype(jnp.bfloat16)
    xg[pl.ds(pl.multiple_of(me * rows, rows), rows), :] = normed

    pl.semaphore_wait(barrier, n - 1 + 2)

    steps = n // 2

    def ag_part(direction, step, c, offset):
        start = at_ring(offset) * rows
        count = rows
        if step == steps:
            start = start + direction * HALF
            count = HALF
        return xg.at[pl.ds(pl.multiple_of(start, count), count), pl.ds(c * chunk, chunk)]

    def ag_copy(direction, step, c):
        sign = 1 - 2 * direction
        index = (direction * steps + step - 1) * CHUNKS + c
        ref = ag_part(direction, step, c, -sign * (step - 1))
        return pltpu.make_async_remote_copy(
            src_ref=ref,
            dst_ref=ref,
            send_sem=ag_send.at[index],
            recv_sem=ag_recv.at[index],
            device_id=(sec, at_ring(sign)),
            device_id_type=MESH,
        )

    def ag_arrived(direction, step, c):
        sign = 1 - 2 * direction
        index = (direction * steps + step - 1) * CHUNKS + c
        ref = ag_part(direction, step, c, -sign * step)
        pltpu.make_async_remote_copy(
            src_ref=ref,
            dst_ref=ref,
            send_sem=ag_send.at[index],
            recv_sem=ag_recv.at[index],
            device_id=(sec, at_ring(sign)),
            device_id_type=MESH,
        ).wait_recv()

    def page_copy(k):
        peer = lax.rem(me + k, n)
        return pltpu.make_async_remote_copy(
            src_ref=pool_hbm.at[:, :, pl.ds(pl.multiple_of(peer * pair, pair), pair)],
            dst_ref=pages.at[pl.ds(me * pool_dev, pool_dev)],
            send_sem=pg_send.at[k],
            recv_sem=pg_recv.at[k],
            device_id=(sec, peer),
            device_id_type=MESH,
        )

    def page_arrived(k):
        peer = lax.rem(me + n - k, n)
        pltpu.make_async_remote_copy(
            src_ref=pool_hbm.at[:, :, pl.ds(pl.multiple_of(me * pair, pair), pair)],
            dst_ref=pages.at[pl.ds(peer * pool_dev, pool_dev)],
            send_sem=pg_send.at[k],
            recv_sem=pg_recv.at[k],
            device_id=(sec, peer),
            device_id_type=MESH,
        ).wait_recv()

    order = sorted(range(1, n), key=lambda k: (abs(k - n // 2), k))
    ag_copies = []
    for c in range(CHUNKS):
        for direction in range(2):
            copy = ag_copy(direction, 1, c)
            copy.start()
            ag_copies.append(copy)
    page_copies = [page_copy(k) for k in order]
    for copy in page_copies:
        copy.start()
    for step in range(2, steps + 1):
        for c in range(CHUNKS):
            for direction in range(2):
                ag_arrived(direction, step - 1, c)
                copy = ag_copy(direction, step, c)
                copy.start()
                ag_copies.append(copy)

    tiles = q_cols // TILE
    for c in range(CHUNKS):
        part = pl.ds(c * chunk, chunk)
        for direction in range(2):
            ag_arrived(direction, steps, c)
        for load in loads[c]:
            load.wait()

        def project(i, carry, c=c, part=part):
            cols = pl.ds(pl.multiple_of(i * TILE, TILE), TILE)
            term = jnp.dot(xg[:, part], wq[part, cols], preferred_element_type=jnp.float32)
            acc[:, cols] = term if c == 0 else acc[:, cols] + term
            return carry

        lax.fori_loop(0, tiles, project, 0)
        term = jnp.dot(xg[:, part], wkv[part, :], preferred_element_type=jnp.float32)
        cols = pl.ds(q_cols, pair)
        acc[:, cols] = term if c == 0 else acc[:, cols] + term

    cosine = cos_ref[...]
    sine = sin_ref[...]
    even = lax.rem(lax.broadcasted_iota(jnp.int32, cosine.shape, 1), 2) == 0

    def turn(values):
        other = jnp.where(even, pltpu.roll(values, HD - 1, 1), pltpu.roll(values, 1, 1))
        return (values * cosine + other * sine).astype(jnp.bfloat16)

    new_rows = REQ * NEW
    key = turn(acc[:, q_cols : q_cols + HD]).reshape(REQ, NEW, HD)
    value = acc[:, q_cols + HD : q_cols + pair].astype(jnp.bfloat16).reshape(REQ, NEW, HD)
    fresh[me, :, :, :HD] = key
    fresh[me, :, :, HD:] = value

    def fresh_copy(k, outgoing):
        peer = lax.rem(me + k, n) if outgoing else lax.rem(me + n - k, n)
        ref = fresh.at[me if outgoing else peer]
        return pltpu.make_async_remote_copy(
            src_ref=ref,
            dst_ref=ref,
            send_sem=kv_send.at[k],
            recv_sem=kv_recv.at[k],
            device_id=(sec, peer),
            device_id_type=MESH,
        )

    fresh_copies = [fresh_copy(k, True) for k in range(1, n)]
    for copy in fresh_copies:
        copy.start()
    for h in range(heads):
        turned = turn(acc[:, h * HD : (h + 1) * HD])
        qs[:, h * NEW : (h + 1) * NEW, :] = turned.reshape(REQ, NEW, HD)

    own_pages.wait()
    for k in order:
        page_arrived(k)

    kbuf[pl.ds(prefix + NEW, NEW), :] = jnp.zeros((NEW, pair), jnp.bfloat16)
    group = heads // 2
    grows = group * NEW
    span = prefix + 2 * NEW
    column = lax.broadcasted_iota(jnp.int32, (grows, span), 1)
    token = lax.rem(lax.broadcasted_iota(jnp.int32, (grows, span), 0), NEW)

    def one_request(r, carry):
        for j in range(listed):
            kbuf[pl.ds(j * PAGE, PAGE), :] = pages[table_ref[r * listed + j]]
        kbuf[pl.ds(prefix, NEW), :] = fresh[me, r]
        limit = jnp.where(column < prefix, lens_ref[r], prefix + 1 + token)
        seen = column < limit
        for part in range(2):
            q = qs[r, part * grows : (part + 1) * grows, :]
            scores = lax.dot_general(
                q, kbuf[:, :HD], (((1,), (1,)), ((), ())), preferred_element_type=jnp.float32
            )
            scores = jnp.where(seen, scores * HD ** (-0.5), -1e30)
            top = jnp.max(scores, axis=-1, keepdims=True)
            expo = jnp.where(seen, jnp.exp(scores - top), 0.0)
            total = jnp.sum(expo, axis=-1, keepdims=True)
            weights = (expo * (1.0 / total)).astype(jnp.bfloat16)
            mixed = jnp.dot(weights, kbuf[:, HD:], preferred_element_type=jnp.float32)
            mixed = mixed.astype(jnp.bfloat16)
            for h in range(group):
                col = (part * group + h) * HD
                att[r, :, col : col + HD] = mixed[h * NEW : (h + 1) * NEW, :]
        return carry

    lax.fori_loop(0, REQ, one_request, 0)

    for copy in ag_copies:
        copy.wait_send()

    def rs_rows(offset):
        return pl.ds(pl.multiple_of(at_ring(offset) * rows, rows), rows)

    def rs_copy(direction, step, c):
        sign = 1 - 2 * direction
        index = (direction * steps + step - 1) * CHUNKS + c
        part = pl.ds(c * chunk, chunk)
        if step == 1:
            start = at_ring(sign * steps) * rows + direction * HALF
            src = xg.at[pl.ds(pl.multiple_of(start, HALF), HALF), part]
            dst = rs_half.at[direction, c]
        else:
            src = xg.at[rs_rows(sign * (steps + 1 - step)), part]
            dst = rs_full.at[direction, step - 2, c]
        return pltpu.make_async_remote_copy(
            src_ref=src,
            dst_ref=dst,
            send_sem=rs_send.at[index],
            recv_sem=rs_recv.at[index],
            device_id=(sec, at_ring(sign)),
            device_id_type=MESH,
        )

    product_tile = min(2 * TILE, chunk)
    rs_copies = {}
    for c in range(CHUNKS):
        out_loads[c].wait()

        def product(i, carry, c=c):
            cols = pl.ds(pl.multiple_of(c * chunk + i * product_tile, product_tile), product_tile)
            xg[:, cols] = jnp.dot(
                att[...].reshape(new_rows, q_cols),
                wo[:, cols],
                preferred_element_type=jnp.float32,
            ).astype(jnp.bfloat16)
            return carry

        lax.fori_loop(0, chunk // product_tile, product, 0)
        for direction in range(2):
            copy = rs_copy(direction, 1, c)
            copy.start()
            rs_copies[direction, 1, c] = copy
    for step in range(2, steps + 1):
        for c in range(CHUNKS):
            part = pl.ds(c * chunk, chunk)
            for direction in range(2):
                sign = 1 - 2 * direction
                rs_copies[direction, step - 1, c].wait_recv()
                if step == 2:
                    start = at_ring(sign * (steps - 1)) * rows + direction * HALF
                    mine = pl.ds(pl.multiple_of(start, HALF), HALF)
                    came = rs_half[direction, c]
                else:
                    mine = rs_rows(sign * (steps + 1 - step))
                    came = rs_full[direction, step - 3, c]
                xg[mine, part] = (
                    xg[mine, part].astype(jnp.float32) + came.astype(jnp.float32)
                ).astype(jnp.bfloat16)
                copy = rs_copy(direction, step, c)
                copy.start()
                rs_copies[direction, step, c] = copy

    hands = []
    own = pl.ds(pl.multiple_of(me * rows, rows), rows)
    for c in range(CHUNKS):
        part = pl.ds(c * chunk, chunk)
        for direction in range(2):
            rs_copies[direction, steps, c].wait_recv()
        summed = xg[own, part].astype(jnp.float32)
        for direction in range(2):
            summed = summed + rs_full[direction, steps - 2, c].astype(jnp.float32)
        block[:, part] = (hidden_ref[:, part].astype(jnp.float32) + summed).astype(jnp.bfloat16)
        hand = pltpu.make_async_remote_copy(
            src_ref=block.at[:, part],
            dst_ref=handed_hbm.at[:, part],
            send_sem=hand_send.at[c],
            recv_sem=hand_recv.at[c],
            device_id=(next_sec, me),
            device_id_type=MESH,
        )
        hand.start()
        hands.append(hand)

    for k in range(1, n):
        fresh_copy(k, False).wait_recv()
    slots = cache_ref.shape[0]
    units = place_ref.shape[0]
    for slot in range(slots):
        wanted = me * slots + slot
        unit = jnp.int32(0)
        for u in range(units):
            unit = jnp.where(place_ref[u] == wanted, u, unit)
        cache_ref[slot] = fresh[lax.rem(unit, KVH), lax.div(unit, KVH)]

    for copy in page_copies:
        copy.wait_send()
    for copy in fresh_copies:
        copy.wait_send()
    for copy in rs_copies.values():
        copy.wait_send()
    for hand in hands:
        hand.wait()


def fused(
    n,
    n_section,
    hidden,
    norm_gain,
    w_query,
    w_keyval,
    w_out,
    kv_pool,
    page_table,
    prefix_len,
    decode_place,
):
    rows, width = hidden.shape
    q_cols = w_query.shape[2]
    pool_dev = kv_pool.shape[1]
    pair = 2 * HD
    new_rows = REQ * NEW
    prefix = page_table.shape[1] // REQ * PAGE
    slots = REQ * KVH // n
    steps = n // 2
    chunk = width // CHUNKS
    heads = q_cols // HD
    lens = prefix_len[0]
    positions = (lens[:, None] + jnp.arange(NEW, dtype=jnp.int32)[None, :]).reshape(-1)
    dims = jnp.arange(HD, dtype=jnp.int32)
    inverse = jnp.power(rope_theta, -(dims // 2 * 2).astype(jnp.float32) / HD)
    angle = positions[:, None].astype(jnp.float32) * inverse[None, :]
    cosine = jnp.cos(angle)
    sine = jnp.where(dims[None, :] % 2 == 0, -jnp.sin(angle), jnp.sin(angle))
    vmem = pl.BlockSpec(memory_space=pltpu.VMEM)
    smem = pl.BlockSpec(memory_space=pltpu.SMEM)
    far = pl.BlockSpec(memory_space=pl.ANY)
    bf16 = jnp.bfloat16
    dma = pltpu.SemaphoreType.DMA
    handed, cache = pl.pallas_call(
        functools.partial(layer_kernel, n, n_section),
        out_shape=(
            jax.ShapeDtypeStruct((rows, width), bf16),
            jax.ShapeDtypeStruct((slots, NEW, pair), bf16),
        ),
        in_specs=[vmem, vmem, far, far, far, far, vmem, vmem, smem, smem, smem],
        out_specs=(far, vmem),
        scratch_shapes=[
            pltpu.VMEM((new_rows, width), bf16),
            pltpu.VMEM((width, q_cols), bf16),
            pltpu.VMEM((width, pair), bf16),
            pltpu.VMEM((q_cols, width), bf16),
            pltpu.VMEM((n * pool_dev, PAGE, pair), bf16),
            pltpu.VMEM((new_rows, q_cols + pair), jnp.float32),
            pltpu.VMEM((REQ, heads * NEW, HD), bf16),
            pltpu.VMEM((n, REQ, NEW, pair), bf16),
            pltpu.VMEM((prefix + 2 * NEW, pair), bf16),
            pltpu.VMEM((REQ, NEW, q_cols), bf16),
            pltpu.VMEM((2, CHUNKS, HALF, chunk), bf16),
            pltpu.VMEM((2, steps - 1, CHUNKS, rows, chunk), bf16),
            pltpu.VMEM((rows, width), bf16),
            dma((3 * CHUNKS,)),
            dma,
            dma((2 * steps * CHUNKS,)),
            dma((2 * steps * CHUNKS,)),
            dma((n,)),
            dma((n,)),
            dma((n,)),
            dma((n,)),
            dma((2 * steps * CHUNKS,)),
            dma((2 * steps * CHUNKS,)),
            dma((CHUNKS,)),
            dma((CHUNKS,)),
        ],
        compiler_params=pltpu.CompilerParams(
            collective_id=0, has_side_effects=True, vmem_limit_bytes=60 * 1024 * 1024
        ),
        cost_estimate=pl.CostEstimate(
            flops=11_000_000_000, bytes_accessed=40_000_000, transcendentals=2_000_000
        ),
    )(
        hidden,
        norm_gain,
        w_query[0],
        w_keyval[0],
        w_out[0],
        kv_pool[0],
        cosine,
        sine,
        page_table[0],
        lens,
        decode_place[0],
    )
    return (handed, cache[None])


def solution(mesh):
    placed = (
        P(("section", "tp"), None),
        P("section", None),
        P("section", None, "tp"),
        P("section", None, "tp"),
        P("section", "tp", None),
        P("section", "tp", None, None),
        P("section", None),
        P("section", None),
        P("section", None),
    )
    n = mesh.shape["tp"]
    body = local
    if n == KVH:
        body = functools.partial(fused, n, mesh.shape["section"])
    return jax.shard_map(
        body,
        mesh=mesh,
        in_specs=placed,
        out_specs=(P(("section", "tp"), None), P("section", "tp", None, None)),
        check_vma=False,
    )
```

profile of v0, /device:TPU:16, one launch (start us, length us, event | category | flops | bytes accessed | tf_op | source)
XLA Modules:
  0.0 167.3 jit_solution(11423691677832022174)
XLA Ops:
  0.7 0.7 add_convert_fusion
  1.4 0.1 convert_element_type.19
  1.5 1.2 negate_select_fusion
  2.7 161.1 %shard_map.104 = (bf16[32,8192]{1,0:T(8,128)(2,1)}, bf16[4,64,256]{2,1,0:T(8,128)(2,1)}) custom-call(bf16[32,8192]{1,0:T(8,128)(2,1)} %hidden_ref.1, f32[1,8192]{1,0:T(1,128)} %gain_ref.1, bf16[8192,1024]{1,0:T(8,128)(2,1)} %bitcast.11, bf16[8192,256]{1,0:T(8,128)(2,1)} %bitcast.13, bf16[1024,8192]{1,0:T(8,128)(2,1)} %bitcast.12, ...), custom_call_target="tpu_custom_call" | custom-call | flops 11000000512 | bytes 40000000 | tf_op jit(solution)/shard_map/pallas_call | solution.py:572
  163.8 1.9 %copy.13 = bf16[32,8192]{1,0:T(8,128)(2,1)} copy(bf16[32,8192]{1,0:T(8,128)(2,1)} %get-tuple-element.10) | data formatting | bytes 1048576
  165.7 1.6 copy.14
  (2 shorter events, 0.0 us)
where the time goes:
time: 167 us
  Pallas kernels  161 us (96%)
  local copies, waits for them, and re-layouts  3.52 us (2%)
  other arithmetic  1.99 us (1%)
    pallas_call x1, Pallas kernels, fused(): pl.pallas_call(functools.partial(layer_kernel, n, n_section), out_shape=(...  161 us
    unnamed x2, local copies, waits for them, and re-layouts  3.44 us

commit v1 on v0

--- a/solution.py
+++ b/solution.py
@@ -176,8 +176,7 @@
     wkv_hbm,
     wo_hbm,
     pool_hbm,
-    cos_ref,
-    sin_ref,
+    inverse_ref,
     table_ref,
     lens_ref,
     place_ref,
@@ -196,6 +195,8 @@
     rs_half,
     rs_full,
     block,
+    cosine,
+    sine,
     w_sem,
     own_sem,
     ag_send,
@@ -264,40 +265,36 @@
     pl.semaphore_wait(barrier, n - 1 + 2)
 
     steps = n // 2
-
-    def ag_part(direction, step, c, offset):
-        start = at_ring(offset) * rows
-        count = rows
-        if step == steps:
-            start = start + direction * HALF
-            count = HALF
-        return xg.at[pl.ds(pl.multiple_of(start, count), count), pl.ds(c * chunk, chunk)]
-
-    def ag_copy(direction, step, c):
-        sign = 1 - 2 * direction
-        index = (direction * steps + step - 1) * CHUNKS + c
-        ref = ag_part(direction, step, c, -sign * (step - 1))
+    line = n // 2
+    z, y = lax.div(me, 2), lax.rem(me, 2)
+
+    def ag_copy(kind, step, c, outgoing):
+        sign = 1 - 2 * (kind % 2)
+        if kind < 2:
+            far = z - sign * (step - 1 if outgoing else step)
+            side = y
+            peer = lax.rem(z + sign + line, line) * 2 + y
+        else:
+            far = z - sign * step
+            side = y if outgoing else 1 - y
+            peer = z * 2 + 1 - y
+        start = (lax.rem(far + line, line) * 2 + side) * rows
+        ref = xg.at[pl.ds(pl.multiple_of(start, rows), rows), pl.ds(c * chunk, chunk)]
+        index = (kind * line + step) * CHUNKS + c
         return pltpu.make_async_remote_copy(
             src_ref=ref,
             dst_ref=ref,
             send_sem=ag_send.at[index],
             recv_sem=ag_recv.at[index],
-            device_id=(sec, at_ring(sign)),
+            device_id=(sec, peer),
             device_id_type=MESH,
         )
 
-    def ag_arrived(direction, step, c):
-        sign = 1 - 2 * direction
-        index = (direction * steps + step - 1) * CHUNKS + c
-        ref = ag_part(direction, step, c, -sign * step)
-        pltpu.make_async_remote_copy(
-            src_ref=ref,
-            dst_ref=ref,
-            send_sem=ag_send.at[index],
-            recv_sem=ag_recv.at[index],
-            device_id=(sec, at_ring(sign)),
-            device_id_type=MESH,
-        ).wait_recv()
+    def holds(kind, step):
+        return z >= step if kind % 2 == 0 else z <= line - 1 - step
+
+    def goes_on(kind):
+        return z <= line - 2 if kind % 2 == 0 else z >= 1
 
     def page_copy(k):
         peer = lax.rem(me + k, n)
@@ -322,28 +319,55 @@
         ).wait_recv()
 
     order = sorted(range(1, n), key=lambda k: (abs(k - n // 2), k))
-    ag_copies = []
     for c in range(CHUNKS):
-        for direction in range(2):
-            copy = ag_copy(direction, 1, c)
-            copy.start()
-            ag_copies.append(copy)
+        for kind in range(2):
+
+            @pl.when(goes_on(kind))
+            def _(kind=kind, c=c):
+                ag_copy(kind, 1, c, True).start()
+
+        ag_copy(2, 0, c, True).start()
     page_copies = [page_copy(k) for k in order]
     for copy in page_copies:
         copy.start()
-    for step in range(2, steps + 1):
+
+    row_ids = lax.broadcasted_iota(jnp.int32, cosine.shape, 0)
+    request = lax.div(row_ids, NEW)
+    position = lax.rem(row_ids, NEW)
+    for r in range(REQ):
+        position = position + jnp.where(request == r, lens_ref[r], 0)
+    even = lax.rem(lax.broadcasted_iota(jnp.int32, cosine.shape, 1), 2) == 0
+    angle = position.astype(jnp.float32) * inverse_ref[...]
+    cosine[...] = jnp.cos(angle)
+    turned_sine = jnp.sin(angle)
+    sine[...] = jnp.where(even, -turned_sine, turned_sine)
+
+    for step in range(1, line):
         for c in range(CHUNKS):
-            for direction in range(2):
-                ag_arrived(direction, step - 1, c)
-                copy = ag_copy(direction, step, c)
-                copy.start()
-                ag_copies.append(copy)
+            for kind in range(2):
+
+                @pl.when(holds(kind, step))
+                def _(kind=kind, step=step, c=c):
+                    ag_copy(kind, step, c, False).wait_recv()
+                    if step < line - 1:
+
+                        @pl.when(goes_on(kind))
+                        def _():
+                            ag_copy(kind, step + 1, c, True).start()
+
+                    ag_copy(kind + 2, step, c, True).start()
 
     tiles = q_cols // TILE
     for c in range(CHUNKS):
         part = pl.ds(c * chunk, chunk)
-        for direction in range(2):
-            ag_arrived(direction, steps, c)
+        ag_copy(2, 0, c, False).wait_recv()
+        for step in range(1, line):
+            for kind in range(2, 4):
+
+                @pl.when(holds(kind, step))
+                def _(kind=kind, step=step, c=c):
+                    ag_copy(kind, step, c, False).wait_recv()
+
         for load in loads[c]:
             load.wait()
 
@@ -358,13 +382,9 @@
         cols = pl.ds(q_cols, pair)
         acc[:, cols] = term if c == 0 else acc[:, cols] + term
 
-    cosine = cos_ref[...]
-    sine = sin_ref[...]
-    even = lax.rem(lax.broadcasted_iota(jnp.int32, cosine.shape, 1), 2) == 0
-
     def turn(values):
         other = jnp.where(even, pltpu.roll(values, HD - 1, 1), pltpu.roll(values, 1, 1))
-        return (values * cosine + other * sine).astype(jnp.bfloat16)
+        return (values * cosine[...] + other * sine[...]).astype(jnp.bfloat16)
 
     new_rows = REQ * NEW
     key = turn(acc[:, q_cols : q_cols + HD]).reshape(REQ, NEW, HD)
@@ -427,8 +447,18 @@
 
     lax.fori_loop(0, REQ, one_request, 0)
 
-    for copy in ag_copies:
-        copy.wait_send()
+    for c in range(CHUNKS):
+        ag_copy(2, 0, c, True).wait_send()
+        for step in range(1, line):
+            for kind in range(2):
+
+                @pl.when(holds(kind, step - 1) & goes_on(kind))
+                def _(kind=kind, step=step, c=c):
+                    ag_copy(kind, step, c, True).wait_send()
+
+                @pl.when(holds(kind, step))
+                def _(kind=kind, step=step, c=c):
+                    ag_copy(kind + 2, step, c, True).wait_send()
 
     def rs_rows(offset):
         return pl.ds(pl.multiple_of(at_ring(offset) * rows, rows), rows)
@@ -558,12 +588,8 @@
     chunk = width // CHUNKS
     heads = q_cols // HD
     lens = prefix_len[0]
-    positions = (lens[:, None] + jnp.arange(NEW, dtype=jnp.int32)[None, :]).reshape(-1)
     dims = jnp.arange(HD, dtype=jnp.int32)
-    inverse = jnp.power(rope_theta, -(dims // 2 * 2).astype(jnp.float32) / HD)
-    angle = positions[:, None].astype(jnp.float32) * inverse[None, :]
-    cosine = jnp.cos(angle)
-    sine = jnp.where(dims[None, :] % 2 == 0, -jnp.sin(angle), jnp.sin(angle))
+    inverse = jnp.power(rope_theta, -(dims // 2 * 2).astype(jnp.float32) / HD)[None, :]
     vmem = pl.BlockSpec(memory_space=pltpu.VMEM)
     smem = pl.BlockSpec(memory_space=pltpu.SMEM)
     far = pl.BlockSpec(memory_space=pl.ANY)
@@ -575,7 +601,7 @@
             jax.ShapeDtypeStruct((rows, width), bf16),
             jax.ShapeDtypeStruct((slots, NEW, pair), bf16),
         ),
-        in_specs=[vmem, vmem, far, far, far, far, vmem, vmem, smem, smem, smem],
+        in_specs=[vmem, vmem, far, far, far, far, vmem, smem, smem, smem],
         out_specs=(far, vmem),
         scratch_shapes=[
             pltpu.VMEM((new_rows, width), bf16),
@@ -591,10 +617,12 @@
             pltpu.VMEM((2, CHUNKS, HALF, chunk), bf16),
             pltpu.VMEM((2, steps - 1, CHUNKS, rows, chunk), bf16),
             pltpu.VMEM((rows, width), bf16),
+            pltpu.VMEM((new_rows, HD), jnp.float32),
+            pltpu.VMEM((new_rows, HD), jnp.float32),
             dma((3 * CHUNKS,)),
             dma,
-            dma((2 * steps * CHUNKS,)),
-            dma((2 * steps * CHUNKS,)),
+            dma((4 * steps * CHUNKS,)),
+            dma((4 * steps * CHUNKS,)),
             dma((n,)),
             dma((n,)),
             dma((n,)),
@@ -617,8 +645,7 @@
         w_keyval[0],
         w_out[0],
         kv_pool[0],
-        cosine,
-        sine,
+        inverse,
         page_table[0],
         lens,
         decode_place[0],

time: 167 us -> 156 us (0.934); the launches traced: 167 us -> 154 us
  Pallas kernels: 161 us -> 150 us
    pallas_call x1, Pallas kernels: 161 us -> 150 us  [fused(): pl.pallas_call(functools.partial(layer_kernel, n, n_section), out_shape=(...]
where the time goes in v1:
time: 156 us; the launch traced here: 154 us
  Pallas kernels  150 us (96%)
  local copies, waits for them, and re-layouts  3.44 us (2%)
    pallas_call x1, Pallas kernels, fused(): pl.pallas_call(functools.partial(layer_kernel, n, n_section), out_shape=(...  150 us
    unnamed x2, local copies, waits for them, and re-layouts  3.44 us

profile of v1, /device:TPU:16, one launch (start us, length us, event | category | flops | bytes accessed | tf_op | source)
XLA Modules:
  0.0 154.3 jit_solution(5673526200740517991)
XLA Ops:
  0.6 0.5 fusion.4.inverse_ref
  1.2 149.7 %shard_map.104 = (bf16[32,8192]{1,0:T(8,128)(2,1)}, bf16[4,64,256]{2,1,0:T(8,128)(2,1)}) custom-call(bf16[32,8192]{1,0:T(8,128)(2,1)} %hidden_ref.1, f32[1,8192]{1,0:T(1,128)} %gain_ref.1, bf16[8192,1024]{1,0:T(8,128)(2,1)} %bitcast.9, bf16[8192,256]{1,0:T(8,128)(2,1)} %bitcast.11, bf16[1024,8192]{1,0:T(8,128)(2,1)} %bitcast.10, ...), custom_call_target="tpu_custom_call" | custom-call | flops 11000000512 | bytes 40000000 | tf_op jit(solution)/shard_map/pallas_call | solution.py:598
  150.9 1.9 %copy.13 = bf16[32,8192]{1,0:T(8,128)(2,1)} copy(bf16[32,8192]{1,0:T(8,128)(2,1)} %get-tuple-element.8) | data formatting | bytes 1048576
  152.7 1.6 %copy.14 = bf16[1,4,64,256]{3,2,1,0:T(8,128)(2,1)} copy(bf16[1,4,64,256]{3,2,1,0:T(8,128)(2,1)} %bitcast.8) | data formatting | bytes 262144

commit v2 on v1

--- a/solution.py
+++ b/solution.py
@@ -318,7 +318,8 @@
             device_id_type=MESH,
         ).wait_recv()
 
-    order = sorted(range(1, n), key=lambda k: (abs(k - n // 2), k))
+    order = sorted(range(1, n), key=lambda k: (k % 2, abs(k - n // 2), k))
+    slots_ahead = [0, 1, 3, 6, 7, 9, 10]
     for c in range(CHUNKS):
         for kind in range(2):
 
@@ -328,8 +329,8 @@
 
         ag_copy(2, 0, c, True).start()
     page_copies = [page_copy(k) for k in order]
-    for copy in page_copies:
-        copy.start()
+    page_copies[0].start()
+    started = 1
 
     row_ids = lax.broadcasted_iota(jnp.int32, cosine.shape, 0)
     request = lax.div(row_ids, NEW)
@@ -357,6 +358,10 @@
 
                     ag_copy(kind + 2, step, c, True).start()
 
+            slot = (step - 1) * CHUNKS + c + 1
+            while started < n - 1 and slots_ahead[started] <= slot:
+                page_copies[started].start()
+                started += 1
     tiles = q_cols // TILE
     for c in range(CHUNKS):
         part = pl.ds(c * chunk, chunk)
@@ -418,27 +423,45 @@
     kbuf[pl.ds(prefix + NEW, NEW), :] = jnp.zeros((NEW, pair), jnp.bfloat16)
     group = heads // 2
     grows = group * NEW
-    span = prefix + 2 * NEW
-    column = lax.broadcasted_iota(jnp.int32, (grows, span), 1)
-    token = lax.rem(lax.broadcasted_iota(jnp.int32, (grows, span), 0), NEW)
+    prefix_column = lax.broadcasted_iota(jnp.int32, (grows, prefix), 1)
+    fresh_column = lax.broadcasted_iota(jnp.int32, (grows, 2 * NEW), 1)
+    token = lax.rem(lax.broadcasted_iota(jnp.int32, (grows, 2 * NEW), 0), NEW)
+    causal = fresh_column <= token
+    factor = HD ** (-0.5) * 1.4426950408889634
+    contract = (((1,), (1,)), ((), ()))
 
     def one_request(r, carry):
         for j in range(listed):
             kbuf[pl.ds(j * PAGE, PAGE), :] = pages[table_ref[r * listed + j]]
         kbuf[pl.ds(prefix, NEW), :] = fresh[me, r]
-        limit = jnp.where(column < prefix, lens_ref[r], prefix + 1 + token)
-        seen = column < limit
+        limit = lens_ref[r]
         for part in range(2):
             q = qs[r, part * grows : (part + 1) * grows, :]
-            scores = lax.dot_general(
-                q, kbuf[:, :HD], (((1,), (1,)), ((), ())), preferred_element_type=jnp.float32
+            old = lax.dot_general(
+                q, kbuf[:prefix, :HD], contract, preferred_element_type=jnp.float32
             )
-            scores = jnp.where(seen, scores * HD ** (-0.5), -1e30)
-            top = jnp.max(scores, axis=-1, keepdims=True)
-            expo = jnp.where(seen, jnp.exp(scores - top), 0.0)
-            total = jnp.sum(expo, axis=-1, keepdims=True)
-            weights = (expo * (1.0 / total)).astype(jnp.bfloat16)
-            mixed = jnp.dot(weights, kbuf[:, HD:], preferred_element_type=jnp.float32)
+            new = lax.dot_general(
+                q, kbuf[prefix:, :HD], contract, preferred_element_type=jnp.float32
+            )
+            old = jnp.where(prefix_column < limit, old, -1e30)
+            new = jnp.where(causal, new, -1e30)
+            top = jnp.maximum(
+                jnp.max(old, axis=-1, keepdims=True), jnp.max(new, axis=-1, keepdims=True)
+            )
+            old = jnp.exp2((old - top) * factor)
+            new = jnp.exp2((new - top) * factor)
+            total = jnp.sum(old, axis=-1, keepdims=True) + jnp.sum(new, axis=-1, keepdims=True)
+            scale = 1.0 / total
+            mixed = jnp.dot(
+                (old * scale).astype(jnp.bfloat16),
+                kbuf[:prefix, HD:],
+                preferred_element_type=jnp.float32,
+            )
+            mixed = mixed + jnp.dot(
+                (new * scale).astype(jnp.bfloat16),
+                kbuf[prefix:, HD:],
+                preferred_element_type=jnp.float32,
+            )
             mixed = mixed.astype(jnp.bfloat16)
             for h in range(group):
                 col = (part * group + h) * HD
@@ -562,6 +585,15 @@
         copy.wait_send()
     for hand in hands:
         hand.wait()
+
+
+def settle_kernel(handed_in, cache_in, handed_out, cache_out, sems):
+    first = pltpu.make_async_copy(handed_in, handed_out, sems.at[0])
+    second = pltpu.make_async_copy(cache_in, cache_out, sems.at[1])
+    first.start()
+    second.start()
+    first.wait()
+    second.wait()
 
 
 def fused(
@@ -650,6 +682,18 @@
         lens,
         decode_place[0],
     )
+    handed, cache = pl.pallas_call(
+        settle_kernel,
+        out_shape=(
+            jax.ShapeDtypeStruct(handed.shape, bf16),
+            jax.ShapeDtypeStruct(cache.shape, bf16),
+        ),
+        in_specs=[far, far],
+        out_specs=(far, far),
+        scratch_shapes=[dma((2,))],
+        compiler_params=pltpu.CompilerParams(vmem_limit_bytes=60 * 1024 * 1024),
+        cost_estimate=pl.CostEstimate(flops=0, bytes_accessed=1_300_000, transcendentals=0),
+    )(handed, cache)
     return (handed, cache[None])
 
 

time: 156 us -> 175 us (1.12)
  Pallas kernels: 150 us -> 171 us
  local copies, waits for them, and re-layouts: 3.44 us -> 0 us
    pallas_call x0 -> x1, Pallas kernels: none -> 21 us  [fused(): pl.pallas_call(settle_kernel, out_shape=(jax.ShapeDtypeStruct(handed.shap...]
    unnamed x2 -> x0, local copies, waits for them, and re-layouts: 3.44 us -> none
where the time goes in v2:
time: 175 us; the launch traced here: 172 us
  Pallas kernels  171 us (98%)
    pallas_call x1, Pallas kernels, fused(): pl.pallas_call(functools.partial(layer_kernel, n, n_section), out_shape=(...  150 us
    pallas_call x1, Pallas kernels, fused(): pl.pallas_call(settle_kernel, out_shape=(jax.ShapeDtypeStruct(handed.shap...  21 us

profile of v2, /device:TPU:16, one launch (start us, length us, event | category | flops | bytes accessed | tf_op | source)
XLA Modules:
  0.0 172.2 jit_solution(18438298767452552170)
XLA Ops:
  0.6 0.5 fusion.4.inverse_ref
  1.2 150.1 %shard_map.104 = (bf16[32,8192]{1,0:T(8,128)(2,1)}, bf16[4,64,256]{2,1,0:T(8,128)(2,1)}) custom-call(bf16[32,8192]{1,0:T(8,128)(2,1)} %hidden_ref.1, f32[1,8192]{1,0:T(1,128)} %gain_ref.1, bf16[8192,1024]{1,0:T(8,128)(2,1)} %bitcast.8, bf16[8192,256]{1,0:T(8,128)(2,1)} %bitcast.10, bf16[1024,8192]{1,0:T(8,128)(2,1)} %bitcast.9, ...), custom_call_target="tpu_custom_call" | custom-call | flops 11000000512 | bytes 40000000 | tf_op jit(solution)/shard_map/pallas_call | solution.py:630
  151.2 21.0 %shard_map.105 = (bf16[32,8192]{1,0:T(8,128)(2,1)}, bf16[4,64,256]{2,1,0:T(8,128)(2,1)}) custom-call(bf16[32,8192]{1,0:T(8,128)(2,1)} %get-tuple-element.6.handed_in, bf16[4,64,256]{2,1,0:T(8,128)(2,1)} %get-tuple-element.7.cache_in), custom_call_target="tpu_custom_call" | custom-call | bytes 1300000 | tf_op jit(solution)/shard_map/pallas_call | solution.py:685

commit v3 on v2

--- a/solution.py
+++ b/solution.py
@@ -180,7 +180,7 @@
     table_ref,
     lens_ref,
     place_ref,
-    handed_hbm,
+    handed_ref,
     cache_ref,
     xg,
     wq,
@@ -197,8 +197,10 @@
     block,
     cosine,
     sine,
+    staged,
     w_sem,
     own_sem,
+    stage_sem,
     ag_send,
     ag_recv,
     pg_send,
@@ -234,6 +236,18 @@
     for other in (next_sec, prev_sec):
         pl.semaphore_signal(barrier, inc=1, device_id=(other, me), device_id_type=MESH)
 
+    pair = 2 * HD
+
+    def page_load(k):
+        peer = lax.rem(me + k, n)
+        return pltpu.make_async_copy(
+            pool_hbm.at[:, :, pl.ds(pl.multiple_of(peer * pair, pair), pair)],
+            staged.at[k],
+            stage_sem.at[k],
+        )
+
+    for k in range(1, n):
+        page_load(k).start()
     loads = []
     for c in range(CHUNKS):
         part = pl.ds(c * chunk, chunk)
@@ -249,7 +263,6 @@
             pltpu.make_async_copy(wo_hbm.at[:, part], wo.at[:, part], w_sem.at[3 * c + 2])
         )
         out_loads[-1].start()
-    pair = 2 * HD
     own_pages = pltpu.make_async_copy(
         pool_hbm.at[:, :, pl.ds(pl.multiple_of(me * pair, pair), pair)],
         pages.at[pl.ds(me * pool_dev, pool_dev)],
@@ -299,7 +312,7 @@
     def page_copy(k):
         peer = lax.rem(me + k, n)
         return pltpu.make_async_remote_copy(
-            src_ref=pool_hbm.at[:, :, pl.ds(pl.multiple_of(peer * pair, pair), pair)],
+            src_ref=staged.at[k],
             dst_ref=pages.at[pl.ds(me * pool_dev, pool_dev)],
             send_sem=pg_send.at[k],
             recv_sem=pg_recv.at[k],
@@ -310,7 +323,7 @@
     def page_arrived(k):
         peer = lax.rem(me + n - k, n)
         pltpu.make_async_remote_copy(
-            src_ref=pool_hbm.at[:, :, pl.ds(pl.multiple_of(me * pair, pair), pair)],
+            src_ref=staged.at[k],
             dst_ref=pages.at[pl.ds(peer * pool_dev, pool_dev)],
             send_sem=pg_send.at[k],
             recv_sem=pg_recv.at[k],
@@ -318,8 +331,7 @@
             device_id_type=MESH,
         ).wait_recv()
 
-    order = sorted(range(1, n), key=lambda k: (k % 2, abs(k - n // 2), k))
-    slots_ahead = [0, 1, 3, 6, 7, 9, 10]
+    order = sorted(range(1, n), key=lambda k: (abs(k - n // 2), k))
     for c in range(CHUNKS):
         for kind in range(2):
 
@@ -329,8 +341,9 @@
 
         ag_copy(2, 0, c, True).start()
     page_copies = [page_copy(k) for k in order]
-    page_copies[0].start()
-    started = 1
+    for k, copy in zip(order, page_copies):
+        page_load(k).wait()
+        copy.start()
 
     row_ids = lax.broadcasted_iota(jnp.int32, cosine.shape, 0)
     request = lax.div(row_ids, NEW)
@@ -358,10 +371,6 @@
 
                     ag_copy(kind + 2, step, c, True).start()
 
-            slot = (step - 1) * CHUNKS + c + 1
-            while started < n - 1 and slots_ahead[started] <= slot:
-                page_copies[started].start()
-                started += 1
     tiles = q_cols // TILE
     for c in range(CHUNKS):
         part = pl.ds(c * chunk, chunk)
@@ -557,7 +566,7 @@
         block[:, part] = (hidden_ref[:, part].astype(jnp.float32) + summed).astype(jnp.bfloat16)
         hand = pltpu.make_async_remote_copy(
             src_ref=block.at[:, part],
-            dst_ref=handed_hbm.at[:, part],
+            dst_ref=handed_ref.at[:, part],
             send_sem=hand_send.at[c],
             recv_sem=hand_recv.at[c],
             device_id=(next_sec, me),
@@ -587,13 +596,9 @@
         hand.wait()
 
 
-def settle_kernel(handed_in, cache_in, handed_out, cache_out, sems):
-    first = pltpu.make_async_copy(handed_in, handed_out, sems.at[0])
-    second = pltpu.make_async_copy(cache_in, cache_out, sems.at[1])
-    first.start()
-    second.start()
-    first.wait()
-    second.wait()
+def settle_kernel(handed_in, cache_in, handed_out, cache_out):
+    handed_out[...] = handed_in[...]
+    cache_out[...] = cache_in[...]
 
 
 def fused(
@@ -634,7 +639,7 @@
             jax.ShapeDtypeStruct((slots, NEW, pair), bf16),
         ),
         in_specs=[vmem, vmem, far, far, far, far, vmem, smem, smem, smem],
-        out_specs=(far, vmem),
+        out_specs=(vmem, vmem),
         scratch_shapes=[
             pltpu.VMEM((new_rows, width), bf16),
             pltpu.VMEM((width, q_cols), bf16),
@@ -651,8 +656,10 @@
             pltpu.VMEM((rows, width), bf16),
             pltpu.VMEM((new_rows, HD), jnp.float32),
             pltpu.VMEM((new_rows, HD), jnp.float32),
+            pltpu.VMEM((n, pool_dev, PAGE, pair), bf16),
             dma((3 * CHUNKS,)),
             dma,
+            dma((n,)),
             dma((4 * steps * CHUNKS,)),
             dma((4 * steps * CHUNKS,)),
             dma((n,)),
@@ -688,9 +695,8 @@
             jax.ShapeDtypeStruct(handed.shape, bf16),
             jax.ShapeDtypeStruct(cache.shape, bf16),
         ),
-        in_specs=[far, far],
-        out_specs=(far, far),
-        scratch_shapes=[dma((2,))],
+        in_specs=[vmem, vmem],
+        out_specs=(vmem, vmem),
         compiler_params=pltpu.CompilerParams(vmem_limit_bytes=60 * 1024 * 1024),
         cost_estimate=pl.CostEstimate(flops=0, bytes_accessed=1_300_000, transcendentals=0),
     )(handed, cache)

time: 175 us -> 154 us (0.88)
  Pallas kernels: 171 us -> 152 us
    pallas_call x1, Pallas kernels: 21 us -> 1.93 us  [fused(): pl.pallas_call(settle_kernel, out_shape=(jax.ShapeDtypeStruct(handed.shap...]
where the time goes in v3:
time: 154 us; the launch traced here: 153 us
  Pallas kernels  152 us (99%)
    pallas_call x1, Pallas kernels, fused(): pl.pallas_call(functools.partial(layer_kernel, n, n_section), out_shape=(...  150 us

profile of v3, /device:TPU:16, one launch (start us, length us, event | category | flops | bytes accessed | tf_op | source)
XLA Modules:
  0.0 152.9 jit_solution(3012801477597860141)
XLA Ops:
  0.6 0.5 fusion.4.inverse_ref
  1.2 149.8 %shard_map.104 = (bf16[32,8192]{1,0:T(8,128)(2,1)}, bf16[4,64,256]{2,1,0:T(8,128)(2,1)}) custom-call(bf16[32,8192]{1,0:T(8,128)(2,1)} %hidden_ref.1, f32[1,8192]{1,0:T(1,128)} %gain_ref.1, bf16[8192,1024]{1,0:T(8,128)(2,1)} %bitcast.8, bf16[8192,256]{1,0:T(8,128)(2,1)} %bitcast.10, bf16[1024,8192]{1,0:T(8,128)(2,1)} %bitcast.9, ...), custom_call_target="tpu_custom_call" | custom-call | flops 11000000512 | bytes 40000000 | tf_op jit(solution)/shard_map/pallas_call | solution.py:635
  151.0 1.9 %shard_map.105 = (bf16[32,8192]{1,0:T(8,128)(2,1)}, bf16[4,64,256]{2,1,0:T(8,128)(2,1)}) custom-call(bf16[32,8192]{1,0:T(8,128)(2,1)} %get-tuple-element.6.handed_in, bf16[4,64,256]{2,1,0:T(8,128)(2,1)} %get-tuple-element.7.cache_in), custom_call_target="tpu_custom_call" | custom-call | bytes 1300000 | tf_op jit(solution)/shard_map/pallas_call | solution.py:692

commit v4 on v3

--- a/solution.py
+++ b/solution.py
@@ -151,7 +151,7 @@
 
 
 MESH = pl.DeviceIdType.MESH
-CHUNKS = 4
+CHUNKS = 8
 TILE = 256
 HALF = 16
 

time: 154 us -> 159 us (1.032)
  Pallas kernels: 152 us -> 156 us
    pallas_call x1, Pallas kernels: 150 us -> 154 us  [fused(): pl.pallas_call(functools.partial(layer_kernel, n, n_section), out_shape=(...]
where the time goes in v4:
time: 159 us; the launch traced here: 157 us
  Pallas kernels  156 us (98%)
    pallas_call x1, Pallas kernels, fused(): pl.pallas_call(functools.partial(layer_kernel, n, n_section), out_shape=(...  154 us

profile of v4, /device:TPU:16, one launch (start us, length us, event | category | flops | bytes accessed | tf_op | source)
XLA Modules:
  0.0 157.4 jit_solution(3173400838774212231)
XLA Ops:
  0.6 0.5 fusion.4.inverse_ref
  1.2 154.3 %shard_map.104 = (bf16[32,8192]{1,0:T(8,128)(2,1)}, bf16[4,64,256]{2,1,0:T(8,128)(2,1)}) custom-call(bf16[32,8192]{1,0:T(8,128)(2,1)} %hidden_ref.1, f32[1,8192]{1,0:T(1,128)} %gain_ref.1, bf16[8192,1024]{1,0:T(8,128)(2,1)} %bitcast.8, bf16[8192,256]{1,0:T(8,128)(2,1)} %bitcast.10, bf16[1024,8192]{1,0:T(8,128)(2,1)} %bitcast.9, ...), custom_call_target="tpu_custom_call" | custom-call | flops 11000000512 | bytes 40000000 | tf_op jit(solution)/shard_map/pallas_call | solution.py:635
  155.5 1.9 %shard_map.105 = (bf16[32,8192]{1,0:T(8,128)(2,1)}, bf16[4,64,256]{2,1,0:T(8,128)(2,1)}) custom-call(bf16[32,8192]{1,0:T(8,128)(2,1)} %get-tuple-element.6.handed_in, bf16[4,64,256]{2,1,0:T(8,128)(2,1)} %get-tuple-element.7.cache_in), custom_call_target="tpu_custom_call" | custom-call | bytes 1300000 | tf_op jit(solution)/shard_map/pallas_call | solution.py:692
